TPU v7x, 32 devices: a whole 2x2x4 slice. The times are simulated.
32 devices in a mesh: win: 4 (over x, core), seq: 8 (over z, y).
Axes of the slice: x: 2, y: 2, z: 4, core: 2. Of those that a mesh axis runs over, the one named last changes fastest.
Arguments:
- embedded: bfloat16 [4, 8192, 768], P('win', 'seq'), may hold values from -6 to 6
- lengths: int32 [4, 4], P('win'), may hold values from 1 to 4096, 8192 in all within a row
- norm_gains: bfloat16 [8, 768], replicated, may hold values from 0.5 to 1.5
- biases: bfloat16 [8, 768], replicated, may hold values from -3 to 3
- conv_taps: bfloat16 [8, 3, 768], replicated, may hold values from -3 to 3
- pointwise: bfloat16 [8, 768, 192], replicated, may hold values from -0.4375 to 0.4375
- channel_order: int32 [8, 768], replicated, may hold values from 0 to 767, each once within a row
Outputs:
- encoded: bfloat16 [4, 8192, 768], P('win', 'seq')
Inputs may be any that keep to these rules, and one draw needn't show every extreme that they name: The lengths of each pack sum to 8192, and some window of each pack has exactly 4096 bins. `channel_order`: each row is a permutation of the 768 channels.
All inputs are finite; a program needn't handle non-finite values.
Results may differ from a plain program's by a relative error of at most 0.015.
Values may be sent and summed in bfloat16 or wider, within the bound.
A program may use at most 64 MiB of HBM per device.

v0:
```python
import functools

import jax
import jax.numpy as jnp
from jax import lax
from jax.experimental import pallas as pl
from jax.experimental.pallas import tpu as pltpu
from jax.sharding import PartitionSpec as P

epsilon = 1e-06
LANES = 128
CHUNK = 128
MXU_ROWS = 256
GELU_C = 0.7978845608028654


def build_weights(pw_ref, order_ref, w_ref, layers):
    channels = w_ref.shape[-1]
    width = pw_ref.shape[-1]

    @pl.loop(0, len(layers))
    def _(i):
        layer = i + layers[0]
        order = order_ref[layer]
        for g in range(channels // width):
            out_ids = lax.broadcasted_iota(jnp.int32, (width, channels), 0) + g * width
            one_hot = jnp.where(out_ids == order, 1.0, 0.0).astype(jnp.bfloat16)
            rows = slice(g * width, (g + 1) * width)
            w_ref[i, rows, :] = jnp.dot(
                pw_ref[layer, rows, :], one_hot, preferred_element_type=jnp.float32
            ).astype(jnp.bfloat16)


def window_rows(len_ref, lo_ref, hi_ref, residue, modulus):
    rows = lo_ref.shape[0]
    pos = lax.broadcasted_iota(jnp.int32, (rows, LANES), 0) * modulus + residue
    wins = len_ref.shape[1]
    total = jnp.int32(0)
    for k in range(wins):
        total = total + len_ref[0, k]
    lo = jnp.zeros((rows, LANES), jnp.int32)
    hi = jnp.zeros((rows, LANES), jnp.int32) + total
    end = jnp.int32(0)
    ends = []
    for k in range(wins):
        end = end + len_ref[0, k]
        ends.append(end)
    for end in ends:
        lo = jnp.where(pos >= end, end, lo)
    for end in reversed(ends):
        hi = jnp.where(pos < end, end, hi)
    lo_ref[...] = pos - lo
    hi_ref[...] = hi - pos


def put_unit(u_ref, pad, start, size, stream):
    mean = jnp.mean(stream * stream, axis=-1, keepdims=True)
    u_ref[pl.ds(pad + start, size), :] = stream * lax.rsqrt(mean + epsilon)


def run_layers(x_ref, y_ref, gain_ref, bias_ref, taps_ref, w_ref, u_ref, act_ref, lo_ref, hi_ref, layers, shifts, modulus):
    rows, channels = x_ref.shape
    pad = (u_ref.shape[0] - rows) // 2
    big = min(MXU_ROWS, rows)

    @pl.loop(0, rows // big)
    def _(i):
        start = pl.multiple_of(i * big, big)
        put_unit(u_ref, pad, start, big, x_ref[pl.ds(start, big), :].astype(jnp.float32))

    for i, layer in enumerate(layers):
        shift = shifts[i]
        source = x_ref if i == 0 else y_ref

        def mix(j, shift=shift, layer=layer):
            at = (lambda n: n) if isinstance(j, int) else (lambda n: pl.multiple_of(n, 8))
            start = j * CHUNK if isinstance(j, int) else pl.multiple_of(j * CHUNK, CHUNK)
            here = pl.ds(start, CHUNK)
            left_ok = lo_ref[here, :] >= shift * modulus
            right_ok = hi_ref[here, :] > shift * modulus
            for k in range(channels // LANES):
                cols = slice(k * LANES, (k + 1) * LANES)
                gain = gain_ref[layer : layer + 1, cols].astype(jnp.float32)
                tap = [gain * taps_ref[layer, t : t + 1, cols].astype(jnp.float32) for t in range(3)]
                bias = bias_ref[layer : layer + 1, cols].astype(jnp.float32)
                v = tap[1] * u_ref[pl.ds(at(start + pad), CHUNK), cols] + bias
                v = v + tap[0] * jnp.where(left_ok, u_ref[pl.ds(at(start + (pad - shift)), CHUNK), cols], 0.0)
                v = v + tap[2] * jnp.where(right_ok, u_ref[pl.ds(at(start + (pad + shift)), CHUNK), cols], 0.0)
                inner = v * (GELU_C + (GELU_C * 0.044715) * (v * v))
                half = 0.5 * v
                act_ref[here, cols] = (half + half * jnp.tanh(inner)).astype(jnp.bfloat16)

        if shift % 8:
            for j in range(rows // CHUNK):
                mix(j)
        else:
            pl.loop(0, rows // CHUNK)(mix)

        @pl.loop(0, rows // big)
        def _(j):
            start = pl.multiple_of(j * big, big)
            here = pl.ds(start, big)
            projected = jnp.dot(act_ref[here, :], w_ref[i], preferred_element_type=jnp.float32)
            fresh = (source[here, :].astype(jnp.float32) + projected).astype(jnp.bfloat16)
            y_ref[here, :] = fresh
            if i + 1 < len(layers):
                put_unit(u_ref, pad, start, big, fresh.astype(jnp.float32))


def stack_kernel(layers, shifts, modulus, held, len_ref, x_ref, gain_ref, bias_ref, taps_ref, pw_ref, order_ref, y_ref, w_ref, u_ref, act_ref, lo_ref, hi_ref):
    h = pl.program_id(0)

    @pl.when(h == 0)
    def _():
        build_weights(pw_ref, order_ref, w_ref, layers)
        u_ref[...] = jnp.zeros_like(u_ref)

    residue = lax.axis_index("seq") * held + h
    window_rows(len_ref, lo_ref, hi_ref, residue, modulus)
    run_layers(x_ref.at[0], y_ref.at[0], gain_ref, bias_ref, taps_ref, w_ref, u_ref, act_ref, lo_ref, hi_ref, layers, shifts, modulus)


def local_stack(x, lengths, gains, biases, taps, pointwise, order, layers, shifts, modulus):
    held, rows, channels = x.shape
    pad = -(-max(shifts) // 8) * 8
    whole = lambda a: pl.BlockSpec(a.shape, lambda h: (0,) * a.ndim)
    order = order.reshape(order.shape[0], 1, channels)
    block = pl.BlockSpec((1, rows, channels), lambda h: (h, 0, 0))
    return pl.pallas_call(
        functools.partial(stack_kernel, layers, shifts, modulus, held),
        grid=(held,),
        out_shape=jax.ShapeDtypeStruct(x.shape, x.dtype),
        in_specs=[pl.BlockSpec(memory_space=pltpu.SMEM), block]
        + [whole(a) for a in (gains, biases, taps, pointwise, order)],
        out_specs=block,
        scratch_shapes=[
            pltpu.VMEM((len(layers), channels, channels), jnp.bfloat16),
            pltpu.VMEM((rows + 2 * pad, channels), jnp.float32),
            pltpu.VMEM((rows, channels), jnp.bfloat16),
            pltpu.VMEM((rows, LANES), jnp.int32),
            pltpu.VMEM((rows, LANES), jnp.int32),
        ],
        compiler_params=pltpu.CompilerParams(vmem_limit_bytes=48 * 2**20),
    )(lengths, x, gains, biases, taps, pointwise, order)


def halo_layer(stream, lengths, gain, bias, taps, weight, order, dilation):
    bins, channels = stream.shape
    count = lax.axis_size("seq")
    pos = lax.axis_index("seq") * bins + jnp.arange(bins, dtype=jnp.int32)
    ends = jnp.cumsum(lengths[0])
    passed = ends[None, :] <= pos[:, None]
    lo = jnp.max(jnp.where(passed, ends[None, :], 0), axis=-1)
    hi = jnp.min(jnp.where(passed, ends[-1], ends[None, :]), axis=-1)
    s = stream.astype(jnp.float32)
    inv = lax.rsqrt(jnp.mean(s * s, axis=-1, keepdims=True) + epsilon)
    normed = (s * inv * gain.astype(jnp.float32)).astype(jnp.bfloat16)
    before = lax.ppermute(normed[-dilation:], "seq", [(i, i + 1) for i in range(count - 1)])
    after = lax.ppermute(normed[:dilation], "seq", [(i + 1, i) for i in range(count - 1)])
    padded = jnp.concatenate([before, normed, after], axis=0).astype(jnp.float32)
    k = taps.astype(jnp.float32)
    v = k[1] * normed.astype(jnp.float32) + bias.astype(jnp.float32)
    v = v + k[0] * jnp.where((pos - dilation >= lo)[:, None], padded[:bins], 0.0)
    v = v + k[2] * jnp.where((pos + dilation < hi)[:, None], padded[2 * dilation :], 0.0)
    act = jax.nn.gelu(v, approximate=True).astype(jnp.bfloat16)
    width = weight.shape[-1]
    groups = channels // width
    projected = jnp.einsum(
        "ngi,gio->ngo",
        act.reshape(bins, groups, width),
        weight.reshape(groups, width, width),
        preferred_element_type=jnp.float32,
    ).reshape(bins, channels)
    return (s + jnp.take(projected, order, axis=-1)).astype(jnp.bfloat16)


def body(embedded, lengths, norm_gains, biases, conv_taps, pointwise, channel_order):
    _, bins, channels = embedded.shape
    layer_count = pointwise.shape[0]
    count = lax.axis_size("seq")
    dilations = [bins * 2**i // 2 ** (layer_count - 2) for i in range(layer_count)]
    modulus = max(count, dilations[0])
    stream = embedded[0]
    first = 0
    while dilations[first] % modulus:
        i = first
        stream = halo_layer(
            stream, lengths, norm_gains[i], biases[i], conv_taps[i], pointwise[i], channel_order[i], dilations[i]
        )
        first += 1
    layers = list(range(first, layer_count))
    shifts = [dilations[i] // modulus for i in layers]
    held = modulus // count
    per = bins // modulus
    x = stream.reshape(per, modulus, channels).transpose(1, 0, 2).reshape(count, held, per, channels)
    x = lax.all_to_all(x, "seq", 0, 0)
    x = x.transpose(1, 0, 2, 3).reshape(held, count * per, channels)
    y = local_stack(x, lengths, norm_gains, biases, conv_taps, pointwise, channel_order, layers, shifts, modulus)
    y = y.reshape(held, count, per, channels).transpose(1, 0, 2, 3)
    y = lax.all_to_all(y, "seq", 0, 0)
    y = y.reshape(modulus, per, channels).transpose(1, 0, 2)
    return y.reshape(1, bins, channels)


def solution(mesh):
    placed = (P("win", "seq", None), P("win", None), P(), P(), P(), P(), P())
    return jax.shard_map(
        body, mesh=mesh, in_specs=placed, out_specs=P("win", "seq", None), check_vma=False
    )
```

profile of v0, /device:TPU:0, one launch (start us, length us, event | category | flops | bytes accessed | tf_op | source)
XLA Modules:
  0.0 135.5 jit_solution(8416159764656215073)
XLA Ops:
  0.0 3.0 %copy.14 = bf16[16,64,768]{2,1,0:T(8,128)(2,1)} copy(bf16[16,64,768]{2,0,1:T(8,128)(2,1)} %bitcast.19) | data formatting | bytes 3145728 | tf_op jit(solution)/shard_map/transpose | solution.py:195
  3.0 0.0 copy-start.4
  3.0 0.0 copy-start.3
  3.0 7.4 %all-to-all-start = ((bf16[8,2,64,768]{3,2,1,0:T(8,128)(2,1)}), bf16[8,2,64,768]{3,2,1,0:T(8,128)(2,1)S(1)}, u32[]{:S(2)}, u32[]{:S(2)}) async-start(bf16[8,2,64,768]{3,2,1,0:T(8,128)(2,1)} %bitcast.2), calls=%async_computation | async-start | bytes 3145728 | tf_op jit(solution)/shard_map/all_to_all | solution.py:196
  10.4 0.0 copy-done.4
  10.5 0.0 copy-done.3
  10.5 4.5 %copy.17.pw_ref = bf16[8,768,192]{2,1,0:T(8,128)(2,1)} copy(bf16[8,768,192]{1,2,0:T(8,128)(2,1)} %param.12) | data formatting | bytes 4718592 | tf_op args[5]
  15.0 32.4 %all-to-all-done = bf16[8,2,64,768]{3,2,1,0:T(8,128)(2,1)S(1)} async-done(((bf16[8,2,64,768]{3,2,1,0:T(8,128)(2,1)}), bf16[8,2,64,768]{3,2,1,0:T(8,128)(2,1)S(1)}, u32[]{:S(2)}, u32[]{:S(2)}) %all-to-all-start) | async-done | bytes 1572896 | tf_op jit(solution)/shard_map/all_to_all | solution.py:196
  47.4 0.0 copy-start
  47.4 0.0 copy-start.1
  47.4 0.0 copy-start.2
  47.4 0.1 copy.15
  47.6 0.6 copy-done
  48.1 0.0 copy-done.1
  48.2 0.0 copy-done.2
  48.2 44.7 %shard_map.73 = bf16[2,512,768]{2,1,0:T(8,128)(2,1)S(1)} custom-call(s32[1,4]{1,0:T(1,128)S(1)} %copy-done.2, bf16[2,512,768]{2,1,0:T(8,128)(2,1)S(1)} %bitcast.14, bf16[8,768]{1,0:T(8,128)(2,1)S(1)} %copy-done, bf16[8,768]{1,0:T(8,128)(2,1)S(1)} %copy-done.1, bf16[8,3,768]{2,1,0:T(4,128)(2,1)S(1)} %copy.16.taps_ref, bf16[8,768,192]{2,1,0:T(8,128)(2,1)} %copy.17.pw_ref, ...), custom_call_target="tpu_custom_call" | custom-call | tf_op jit(solution)/shard_map/pallas_call | solution.py:129
  92.8 0.1 copy.21
  93.0 40.6 %all_to_all.10 = bf16[8,2,64,768]{3,2,1,0:T(8,128)(2,1)S(1)} all-to-all(bf16[8,2,64,768]{3,2,1,0:T(8,128)(2,1)S(1)} %bitcast.17), channel_id=1, replica_groups=mesh['win'=4,'seq'=8] {'seq'}, dimensions={0} | all-to-all | bytes 3145728 | tf_op jit(solution)/shard_map/all_to_all | solution.py:200
  133.5 2.0 %copy.19 = bf16[64,16,768]{2,1,0:T(8,128)(2,1)} copy(bf16[64,16,768]{2,0,1:T(8,128)(2,1)S(1)} %bitcast.18) | data formatting | bytes 3145728 | tf_op jit(solution)/shard_map/transpose | solution.py:201
  (2 shorter events, 0.0 us)
Async XLA Ops:
  3.0 7.4 %copy-start.4 = (s32[8,768]{1,0:T(8,128)S(1)}, s32[8,768]{1,0:T(8,128)}, u32[]{:S(2)}) copy-start(s32[8,768]{1,0:T(8,128)} %param.13) | copy-start | bytes 73732
  3.0 7.4 %copy-start.3 = (bf16[8,3,768]{2,0,1:T(8,128)(2,1)S(1)}, bf16[8,3,768]{2,0,1:T(8,128)(2,1)}, u32[]{:S(2)}) copy-start(bf16[8,3,768]{2,0,1:T(8,128)(2,1)} %param.11) | copy-start | bytes 110596
  3.0 44.4 %all-to-all-start = ((bf16[8,2,64,768]{3,2,1,0:T(8,128)(2,1)}), bf16[8,2,64,768]{3,2,1,0:T(8,128)(2,1)S(1)}, u32[]{:S(2)}, u32[]{:S(2)}) async-start(bf16[8,2,64,768]{3,2,1,0:T(8,128)(2,1)} %bitcast.2), calls=%async_computation | async-start | bytes 3145728 | tf_op jit(solution)/shard_map/all_to_all | solution.py:196
  47.4 0.7 copy-start
  47.4 0.7 copy-start.1
  47.4 0.7 copy-start.2
where the time goes:
time: 136 us
  Pallas kernels  44.7 us (33%)
  blocking collectives  40.6 us (30%)
  waiting for transfers between devices  32.4 us (24%)
  local copies, waits for them, and re-layouts  10.4 us (8%)
  starting transfers between devices  7.41 us (5%)
    pallas_call x1, Pallas kernels, local_stack(): pl.pallas_call(functools.partial(stack_kernel, layers, shifts, modulus, h...  44.7 us
    all_to_all x1, blocking collectives, body(): y = lax.all_to_all(y, 'seq', 0, 0)  40.6 us
    all_to_all x1, waiting for transfers between devices, body(): x = lax.all_to_all(x, 'seq', 0, 0)  32.4 us
    all_to_all x1, starting transfers between devices, body(): x = lax.all_to_all(x, 'seq', 0, 0)  7.41 us
    unnamed x12, local copies, waits for them, and re-layouts  5.14 us
    transpose x1, local copies, waits for them, and re-layouts, body(): stream.reshape(per, modulus, channels).transpose(1, 0, 2)  3.02 us
  transfers between devices with their start and end apart: 1, of which 1 were waited for; matrix products, arithmetic and copies ran while one was open for 3% of the time, Pallas kernels for 0%

commit v1 on v0

--- a/solution.py
+++ b/solution.py
@@ -58,7 +58,7 @@
     u_ref[pl.ds(pad + start, size), :] = stream * lax.rsqrt(mean + epsilon)
 
 
-def run_layers(x_ref, y_ref, gain_ref, bias_ref, taps_ref, w_ref, u_ref, act_ref, lo_ref, hi_ref, layers, shifts, modulus):
+def run_layers(x_ref, y_ref, gain_ref, bias_ref, taps_ref, w_ref, u_ref, act_ref, lo_ref, hi_ref, layers, shifts, modulus, copies):
     rows, channels = x_ref.shape
     pad = (u_ref.shape[0] - rows) // 2
     big = min(MXU_ROWS, rows)
@@ -95,6 +95,7 @@
                 mix(j)
         else:
             pl.loop(0, rows // CHUNK)(mix)
+        copies[i].wait()
 
         @pl.loop(0, rows // big)
         def _(j):
@@ -107,41 +108,55 @@
                 put_unit(u_ref, pad, start, big, fresh.astype(jnp.float32))
 
 
-def stack_kernel(layers, shifts, modulus, held, len_ref, x_ref, gain_ref, bias_ref, taps_ref, pw_ref, order_ref, y_ref, w_ref, u_ref, act_ref, lo_ref, hi_ref):
-    h = pl.program_id(0)
-
-    @pl.when(h == 0)
-    def _():
-        build_weights(pw_ref, order_ref, w_ref, layers)
-        u_ref[...] = jnp.zeros_like(u_ref)
-
-    residue = lax.axis_index("seq") * held + h
-    window_rows(len_ref, lo_ref, hi_ref, residue, modulus)
-    run_layers(x_ref.at[0], y_ref.at[0], gain_ref, bias_ref, taps_ref, w_ref, u_ref, act_ref, lo_ref, hi_ref, layers, shifts, modulus)
-
-
-def local_stack(x, lengths, gains, biases, taps, pointwise, order, layers, shifts, modulus):
-    held, rows, channels = x.shape
+def weights_kernel(layers, pw_ref, order_ref, w_ref):
+    build_weights(pw_ref, order_ref, w_ref, layers)
+
+
+def dense_weights(pointwise, order, layers):
+    channels = pointwise.shape[1]
+    in_vmem = pl.BlockSpec(memory_space=pltpu.VMEM)
+    return pl.pallas_call(
+        functools.partial(weights_kernel, layers),
+        out_shape=jax.ShapeDtypeStruct((len(layers), channels, channels), pointwise.dtype),
+        in_specs=[in_vmem] * 2,
+        out_specs=in_vmem,
+        cost_estimate=pl.CostEstimate(flops=2 * 10**9, bytes_accessed=2 * 10**7, transcendentals=0),
+        compiler_params=pltpu.CompilerParams(vmem_limit_bytes=12 * 2**20),
+    )(pointwise, order.reshape(order.shape[0], 1, channels))
+
+
+def stack_kernel(layers, shifts, modulus, base, len_ref, x_ref, gain_ref, bias_ref, taps_ref, w_hbm, y_ref, u_ref, act_ref, lo_ref, hi_ref, w_ref, sems):
+    copies = [pltpu.make_async_copy(w_hbm.at[i], w_ref.at[i], sems.at[i]) for i in range(len(layers))]
+    for copy in copies:
+        copy.start()
+    pad = (u_ref.shape[0] - x_ref.shape[0]) // 2
+    edge = jnp.zeros((pad, u_ref.shape[1]), u_ref.dtype)
+    u_ref[:pad, :] = edge
+    u_ref[u_ref.shape[0] - pad :, :] = edge
+    window_rows(len_ref, lo_ref, hi_ref, lax.axis_index("seq") + base, modulus)
+    run_layers(x_ref, y_ref, gain_ref, bias_ref, taps_ref, w_ref, u_ref, act_ref, lo_ref, hi_ref, layers, shifts, modulus, copies)
+
+
+def local_stack(x, lengths, gains, biases, taps, weights, layers, shifts, modulus, base):
+    rows, channels = x.shape
     pad = -(-max(shifts) // 8) * 8
-    whole = lambda a: pl.BlockSpec(a.shape, lambda h: (0,) * a.ndim)
-    order = order.reshape(order.shape[0], 1, channels)
-    block = pl.BlockSpec((1, rows, channels), lambda h: (h, 0, 0))
+    in_vmem = pl.BlockSpec(memory_space=pltpu.VMEM)
     return pl.pallas_call(
-        functools.partial(stack_kernel, layers, shifts, modulus, held),
-        grid=(held,),
+        functools.partial(stack_kernel, layers, shifts, modulus, base),
         out_shape=jax.ShapeDtypeStruct(x.shape, x.dtype),
-        in_specs=[pl.BlockSpec(memory_space=pltpu.SMEM), block]
-        + [whole(a) for a in (gains, biases, taps, pointwise, order)],
-        out_specs=block,
+        in_specs=[pl.BlockSpec(memory_space=pltpu.SMEM)] + [in_vmem] * 4 + [pl.BlockSpec(memory_space=pltpu.HBM)],
+        out_specs=in_vmem,
         scratch_shapes=[
-            pltpu.VMEM((len(layers), channels, channels), jnp.bfloat16),
             pltpu.VMEM((rows + 2 * pad, channels), jnp.float32),
             pltpu.VMEM((rows, channels), jnp.bfloat16),
             pltpu.VMEM((rows, LANES), jnp.int32),
             pltpu.VMEM((rows, LANES), jnp.int32),
+            pltpu.VMEM(weights.shape, weights.dtype),
+            pltpu.SemaphoreType.DMA((len(layers),)),
         ],
-        compiler_params=pltpu.CompilerParams(vmem_limit_bytes=48 * 2**20),
-    )(lengths, x, gains, biases, taps, pointwise, order)
+        cost_estimate=pl.CostEstimate(flops=2 * 10**10, bytes_accessed=2 * 10**7, transcendentals=0),
+        compiler_params=pltpu.CompilerParams(vmem_limit_bytes=56 * 2**20),
+    )(lengths, x, gains, biases, taps, weights)
 
 
 def halo_layer(stream, lengths, gain, bias, taps, weight, order, dilation):
@@ -192,13 +207,26 @@
     shifts = [dilations[i] // modulus for i in layers]
     held = modulus // count
     per = bins // modulus
-    x = stream.reshape(per, modulus, channels).transpose(1, 0, 2).reshape(count, held, per, channels)
-    x = lax.all_to_all(x, "seq", 0, 0)
-    x = x.transpose(1, 0, 2, 3).reshape(held, count * per, channels)
-    y = local_stack(x, lengths, norm_gains, biases, conv_taps, pointwise, channel_order, layers, shifts, modulus)
-    y = y.reshape(held, count, per, channels).transpose(1, 0, 2, 3)
-    y = lax.all_to_all(y, "seq", 0, 0)
-    y = y.reshape(modulus, per, channels).transpose(1, 0, 2)
+    weights = dense_weights(pointwise, channel_order, layers)
+    spread = stream.reshape(per, modulus, channels)
+    back = []
+    arrived = None
+    for h in range(held):
+        part = spread[:, h * count : (h + 1) * count].transpose(1, 0, 2)
+        if arrived is not None:
+            part, arrived = lax.optimization_barrier((part, arrived))
+            back.append(arrived)
+        arrived = lax.all_to_all(part, "seq", 0, 0)
+    back.append(arrived)
+    done = None
+    outs = []
+    for h in range(held):
+        x = back[h].reshape(count * per, channels)
+        if done is not None:
+            outs.append(lax.all_to_all(done.reshape(count, per, channels), "seq", 0, 0))
+        done = local_stack(x, lengths, norm_gains, biases, conv_taps, weights, layers, shifts, modulus, h * count)
+    outs.append(lax.all_to_all(done.reshape(count, per, channels), "seq", 0, 0))
+    y = jnp.concatenate([o.transpose(1, 0, 2) for o in outs], axis=1)
     return y.reshape(1, bins, channels)
 
 

time: 136 us -> 111 us (0.82)
  waiting for transfers between devices: 32.4 us -> 8.08 us
  blocking collectives: 40.6 us -> 25.2 us
  starting transfers between devices: 7.41 us -> 16.8 us
  local copies, waits for them, and re-layouts: 10.4 us -> 12.9 us
  Pallas kernels: 44.7 us -> 47 us
    all_to_all x1 -> x3, waiting for transfers between devices: 32.4 us -> 8.08 us  [the longest x2 8.08 us: body(): arrived = lax.all_to_all(part, 'seq', 0, 0)]
    all_to_all x1, blocking collectives: 40.6 us -> 25.2 us  [body(): outs.append(lax.all_to_all(done.reshape(count, per, channels), 'seq', 0, 0))]
    all_to_all x1 -> x3, starting transfers between devices: 7.41 us -> 16.8 us  [the longest x2 10.8 us: body(): arrived = lax.all_to_all(part, 'seq', 0, 0)]
    transpose x3 -> x0, local copies, waits for them, and re-layouts: 5.13 us -> none  [the longest x1 3.02 us: body(): stream.reshape(per, modulus, channels).transpose(1, 0, 2)]
    unnamed x12, local copies, waits for them, and re-layouts: 5.14 us -> 9.37 us
    pallas_call x1 -> x3, Pallas kernels: 44.7 us -> 47 us  [the longest x2 43.1 us: local_stack(): pl.pallas_call(functools.partial(stack_kernel, layers, shifts, modulus, b...]
    concatenate x0 -> x1, local copies, waits for them, and re-layouts: none -> 2.01 us  [body(): y = jnp.concatenate([o.transpose(1, 0, 2) for o in outs], axis=1)]
    slice x0 -> x1, local copies, waits for them, and re-layouts: none -> 1.47 us  [body(): part = spread[:, h * count:(h + 1) * count].transpose(1, 0, 2)]
  transfers between devices with their start and end apart: 1 -> 3, of which waited for: 1 -> 1; matrix products, arithmetic and copies ran while one was open for 3% -> 4% of each run, Pallas kernels for 0% -> 43%
where the time goes in v1:
time: 111 us; the launch traced here: 110 us
  Pallas kernels  47 us (42%)
  blocking collectives  25.2 us (23%)
  starting transfers between devices  16.8 us (15%)
  local copies, waits for them, and re-layouts  12.9 us (12%)
  waiting for transfers between devices  8.08 us (7%)
    pallas_call x2, Pallas kernels, local_stack(): pl.pallas_call(functools.partial(stack_kernel, layers, shifts, modulus, b...  43.1 us
    all_to_all x1, blocking collectives, body(): outs.append(lax.all_to_all(done.reshape(count, per, channels), 'seq', 0, 0))  25.2 us
    all_to_all x2, starting transfers between devices, body(): arrived = lax.all_to_all(part, 'seq', 0, 0)  10.8 us
    unnamed x12, local copies, waits for them, and re-layouts  9.37 us
    all_to_all x2, waiting for transfers between devices, body(): arrived = lax.all_to_all(part, 'seq', 0, 0)  8.08 us
    all_to_all x1, starting transfers between devices, body(): outs.append(lax.all_to_all(done.reshape(count, per, channels), 'seq', 0, 0))  6.01 us
    pallas_call x1, Pallas kernels, dense_weights(): pl.pallas_call(functools.partial(weights_kernel, layers), out_shape=jax.S...  3.83 us
  transfers between devices with their start and end apart: 3, of which 1 were waited for; matrix products, arithmetic and copies ran while one was open for 4% of the time, Pallas kernels for 43%

profile of v1, /device:TPU:0, one launch (start us, length us, event | category | flops | bytes accessed | tf_op | source)
XLA Modules:
  0.0 110.2 jit_solution(10711911343546592709)
XLA Ops:
  0.0 1.5 %fusion = (bf16[64,8,768]{2,1,0:T(8,128)(2,1)S(1)}, bf16[64,8,768]{2,1,0:T(8,128)(2,1)S(1)}) fusion(bf16[64,16,768]{2,1,0:T(8,128)(2,1)} %bitcast.17), kind=kLoop, calls=%fused_computation.3 | loop fusion | bytes 3145728 | tf_op jit(solution)/shard_map/slice | solution.py:215
  1.5 1.0 copy.18
  2.5 7.3 %all-to-all-start = ((bf16[8,64,768]{2,1,0:T(8,128)(2,1)}), bf16[8,64,768]{2,1,0:T(8,128)(2,1)}, u32[]{:S(2)}, u32[]{:S(2)}) async-start(bf16[8,64,768]{2,1,0:T(8,128)(2,1)} %bitcast.12), calls=%async_computation | async-start | bytes 1572864 | tf_op jit(solution)/shard_map/all_to_all | solution.py:219
  9.8 1.0 copy.19
  10.8 0.0 copy-start.3
  10.8 0.0 copy-start.2
  10.8 3.0 %copy.10.pw_ref = bf16[8,768,192]{2,1,0:T(8,128)(2,1)S(1)} copy(bf16[8,768,192]{1,2,0:T(8,128)(2,1)} %param.12) | data formatting | bytes 4718592 | tf_op args[5]
  13.9 0.0 copy-done.3
  13.9 0.0 copy-done.2
  13.9 0.6 copy.11.taps_ref
  14.5 3.8 %shard_map.73.w_hbm = bf16[8,768,768]{2,1,0:T(8,128)(2,1)S(1)} custom-call(bf16[8,768,192]{2,1,0:T(8,128)(2,1)S(1)} %copy.10.pw_ref, s32[8,1,768]{2,1,0:T(1,128)S(1)} %reshape.19.order_ref), custom_call_target="tpu_custom_call" | custom-call | flops 2000000000 | bytes 20000000 | tf_op jit(solution)/shard_map/pallas_call | solution.py:118
  18.4 0.0 copy-start
  18.4 3.6 %copy-done = bf16[8,768,768]{2,1,0:T(8,128)(2,1)} copy-done((bf16[8,768,768]{2,1,0:T(8,128)(2,1)}, bf16[8,768,768]{2,1,0:T(8,128)(2,1)S(1)}, u32[]{:S(2)}) %copy-start) | copy-done | bytes 9437208
  22.0 8.1 %all-to-all-done = bf16[8,64,768]{2,1,0:T(8,128)(2,1)} async-done(((bf16[8,64,768]{2,1,0:T(8,128)(2,1)}), bf16[8,64,768]{2,1,0:T(8,128)(2,1)}, u32[]{:S(2)}, u32[]{:S(2)}) %all-to-all-start) | async-done | bytes 786464 | tf_op jit(solution)/shard_map/all_to_all | solution.py:219
  30.1 3.6 %all-to-all-start.2 = ((bf16[8,64,768]{2,1,0:T(8,128)(2,1)}), bf16[8,64,768]{2,1,0:T(8,128)(2,1)S(1)}, u32[]{:S(2)}, u32[]{:S(2)}) async-start(bf16[8,64,768]{2,1,0:T(8,128)(2,1)} %bitcast.14), calls=%async_computation.2 | async-start | bytes 1572864 | tf_op jit(solution)/shard_map/all_to_all | solution.py:219
  33.6 21.6 %shard_map.74 = bf16[512,768]{1,0:T(8,128)(2,1)} custom-call(s32[1,4]{1,0:T(1,128)} %len_ref.3, bf16[512,768]{1,0:T(8,128)(2,1)} %bitcast.3.x_ref, bf16[8,768]{1,0:T(8,128)(2,1)} %gain_ref.3, bf16[8,768]{1,0:T(8,128)(2,1)} %bias_ref.3, bf16[8,3,768]{2,1,0:T(4,128)(2,1)} %copy.11.taps_ref, bf16[8,768,768]{2,1,0:T(8,128)(2,1)} %copy-done), custom_call_target="tpu_custom_call" | custom-call | flops 20000000000 | bytes 20000000 | tf_op jit(solution)/shard_map/pallas_call | solution.py:144
  55.2 0.0 all-to-all-done.2
  55.2 0.0 copy-start.1
  55.3 6.0 %all-to-all-start.1 = ((bf16[8,64,768]{2,1,0:T(8,128)(2,1)}), bf16[8,64,768]{2,1,0:T(8,128)(2,1)S(1)}, u32[]{:S(2)}, u32[]{:S(2)}) async-start(bf16[8,64,768]{2,1,0:T(8,128)(2,1)} %bitcast.19), calls=%async_computation.1 | async-start | bytes 1572864 | tf_op jit(solution)/shard_map/all_to_all | solution.py:226
  61.3 0.0 copy-done.1
  61.3 21.6 %shard_map.75 = bf16[512,768]{1,0:T(8,128)(2,1)} custom-call(s32[1,4]{1,0:T(1,128)} %len_ref.3, bf16[512,768]{1,0:T(8,128)(2,1)} %bitcast.18, bf16[8,768]{1,0:T(8,128)(2,1)} %gain_ref.3, bf16[8,768]{1,0:T(8,128)(2,1)} %bias_ref.3, bf16[8,3,768]{2,1,0:T(4,128)(2,1)} %copy.11.taps_ref, bf16[8,768,768]{2,1,0:T(8,128)(2,1)} %copy-done), custom_call_target="tpu_custom_call" | custom-call | flops 20000000000 | bytes 20000000 | tf_op jit(solution)/shard_map/pallas_call | solution.py:144
  82.8 0.0 all-to-all-done.1
  82.9 25.2 %all_to_all.20 = bf16[8,64,768]{2,1,0:T(8,128)(2,1)S(1)} all-to-all(bf16[8,64,768]{2,1,0:T(8,128)(2,1)} %bitcast.20), channel_id=1, replica_groups=mesh['win'=4,'seq'=8] {'seq'}, dimensions={0} | all-to-all | bytes 1572864 | tf_op jit(solution)/shard_map/all_to_all | solution.py:228
  108.1 0.1 pad_maximum_fusion
  108.2 2.0 %copy.13 = bf16[64,16,768]{2,1,0:T(8,128)(2,1)} copy(bf16[64,16,768]{2,0,1:T(8,128)(2,1)S(1)} %pad_maximum_fusion) | data formatting | bytes 3145728 | tf_op jit(solution)/shard_map/concatenate | solution.py:229
  (1 shorter events, 0.0 us)
Async XLA Ops:
  2.5 27.6 %all-to-all-start = ((bf16[8,64,768]{2,1,0:T(8,128)(2,1)}), bf16[8,64,768]{2,1,0:T(8,128)(2,1)}, u32[]{:S(2)}, u32[]{:S(2)}) async-start(bf16[8,64,768]{2,1,0:T(8,128)(2,1)} %bitcast.12), calls=%async_computation | async-start | bytes 1572864 | tf_op jit(solution)/shard_map/all_to_all | solution.py:219
  10.8 3.0 %copy-start.3 = (s32[8,768]{1,0:T(8,128)S(1)}, s32[8,768]{1,0:T(8,128)}, u32[]{:S(2)}) copy-start(s32[8,768]{1,0:T(8,128)} %param.13) | copy-start | bytes 73732
  10.8 3.1 %copy-start.2 = (bf16[8,3,768]{2,0,1:T(8,128)(2,1)S(1)}, bf16[8,3,768]{2,0,1:T(8,128)(2,1)}, u32[]{:S(2)}) copy-start(bf16[8,3,768]{2,0,1:T(8,128)(2,1)} %param.11) | copy-start | bytes 110596
  18.4 3.6 %copy-start = (bf16[8,768,768]{2,1,0:T(8,128)(2,1)}, bf16[8,768,768]{2,1,0:T(8,128)(2,1)S(1)}, u32[]{:S(2)}) copy-start(bf16[8,768,768]{2,1,0:T(8,128)(2,1)S(1)} %shard_map.73.w_hbm) | copy-start | bytes 28311556
  30.1 25.1 %all-to-all-start.2 = ((bf16[8,64,768]{2,1,0:T(8,128)(2,1)}), bf16[8,64,768]{2,1,0:T(8,128)(2,1)S(1)}, u32[]{:S(2)}, u32[]{:S(2)}) async-start(bf16[8,64,768]{2,1,0:T(8,128)(2,1)} %bitcast.14), calls=%async_computation.2 | async-start | bytes 1572864 | tf_op jit(solution)/shard_map/all_to_all | solution.py:219
  55.2 6.0 %copy-start.1 = (bf16[8,64,768]{2,1,0:T(8,128)(2,1)}, bf16[8,64,768]{2,1,0:T(8,128)(2,1)S(1)}, u32[]{:S(2)}) copy-start(bf16[8,64,768]{2,1,0:T(8,128)(2,1)S(1)} %all-to-all-done.2) | copy-start | bytes 2359300
  55.3 27.6 %all-to-all-start.1 = ((bf16[8,64,768]{2,1,0:T(8,128)(2,1)}), bf16[8,64,768]{2,1,0:T(8,128)(2,1)S(1)}, u32[]{:S(2)}, u32[]{:S(2)}) async-start(bf16[8,64,768]{2,1,0:T(8,128)(2,1)} %bitcast.19), calls=%async_computation.1 | async-start | bytes 1572864 | tf_op jit(solution)/shard_map/all_to_all | solution.py:226

commit v2 on v1

--- a/solution.py
+++ b/solution.py
@@ -60,19 +60,21 @@
 
 def run_layers(x_ref, y_ref, gain_ref, bias_ref, taps_ref, w_ref, u_ref, act_ref, lo_ref, hi_ref, layers, shifts, modulus, copies):
     rows, channels = x_ref.shape
-    pad = (u_ref.shape[0] - rows) // 2
+    pad = (u_ref.shape[1] - rows) // 2
     big = min(MXU_ROWS, rows)
+    straight = rows <= 2 * MXU_ROWS
 
     @pl.loop(0, rows // big)
     def _(i):
         start = pl.multiple_of(i * big, big)
-        put_unit(u_ref, pad, start, big, x_ref[pl.ds(start, big), :].astype(jnp.float32))
+        put_unit(u_ref.at[0], pad, start, big, x_ref[pl.ds(start, big), :].astype(jnp.float32))
 
     for i, layer in enumerate(layers):
         shift = shifts[i]
         source = x_ref if i == 0 else y_ref
-
-        def mix(j, shift=shift, layer=layer):
+        now, later = u_ref.at[i % 2], u_ref.at[(i + 1) % 2]
+
+        def mix(j, shift=shift, layer=layer, now=now):
             at = (lambda n: n) if isinstance(j, int) else (lambda n: pl.multiple_of(n, 8))
             start = j * CHUNK if isinstance(j, int) else pl.multiple_of(j * CHUNK, CHUNK)
             here = pl.ds(start, CHUNK)
@@ -83,29 +85,35 @@
                 gain = gain_ref[layer : layer + 1, cols].astype(jnp.float32)
                 tap = [gain * taps_ref[layer, t : t + 1, cols].astype(jnp.float32) for t in range(3)]
                 bias = bias_ref[layer : layer + 1, cols].astype(jnp.float32)
-                v = tap[1] * u_ref[pl.ds(at(start + pad), CHUNK), cols] + bias
-                v = v + tap[0] * jnp.where(left_ok, u_ref[pl.ds(at(start + (pad - shift)), CHUNK), cols], 0.0)
-                v = v + tap[2] * jnp.where(right_ok, u_ref[pl.ds(at(start + (pad + shift)), CHUNK), cols], 0.0)
+                v = tap[1] * now[pl.ds(at(start + pad), CHUNK), cols] + bias
+                v = v + tap[0] * jnp.where(left_ok, now[pl.ds(at(start + (pad - shift)), CHUNK), cols], 0.0)
+                v = v + tap[2] * jnp.where(right_ok, now[pl.ds(at(start + (pad + shift)), CHUNK), cols], 0.0)
                 inner = v * (GELU_C + (GELU_C * 0.044715) * (v * v))
                 half = 0.5 * v
                 act_ref[here, cols] = (half + half * jnp.tanh(inner)).astype(jnp.bfloat16)
 
-        if shift % 8:
-            for j in range(rows // CHUNK):
-                mix(j)
-        else:
-            pl.loop(0, rows // CHUNK)(mix)
-        copies[i].wait()
-
-        @pl.loop(0, rows // big)
-        def _(j):
-            start = pl.multiple_of(j * big, big)
+        def project(j, i=i, source=source, later=later):
+            start = j * big if isinstance(j, int) else pl.multiple_of(j * big, big)
             here = pl.ds(start, big)
             projected = jnp.dot(act_ref[here, :], w_ref[i], preferred_element_type=jnp.float32)
             fresh = (source[here, :].astype(jnp.float32) + projected).astype(jnp.bfloat16)
             y_ref[here, :] = fresh
             if i + 1 < len(layers):
-                put_unit(u_ref, pad, start, big, fresh.astype(jnp.float32))
+                put_unit(later, pad, start, big, fresh.astype(jnp.float32))
+
+        copies[i].wait()
+        if straight:
+            for j in range(rows // big):
+                for k in range(big // CHUNK):
+                    mix(j * (big // CHUNK) + k)
+                project(j)
+        else:
+            if shift % 8:
+                for j in range(rows // CHUNK):
+                    mix(j)
+            else:
+                pl.loop(0, rows // CHUNK)(mix)
+            pl.loop(0, rows // big)(project)
 
 
 def weights_kernel(layers, pw_ref, order_ref, w_ref):
@@ -129,10 +137,10 @@
     copies = [pltpu.make_async_copy(w_hbm.at[i], w_ref.at[i], sems.at[i]) for i in range(len(layers))]
     for copy in copies:
         copy.start()
-    pad = (u_ref.shape[0] - x_ref.shape[0]) // 2
-    edge = jnp.zeros((pad, u_ref.shape[1]), u_ref.dtype)
-    u_ref[:pad, :] = edge
-    u_ref[u_ref.shape[0] - pad :, :] = edge
+    pad = (u_ref.shape[1] - x_ref.shape[0]) // 2
+    edge = jnp.zeros((2, pad, u_ref.shape[2]), u_ref.dtype)
+    u_ref[:, :pad, :] = edge
+    u_ref[:, u_ref.shape[1] - pad :, :] = edge
     window_rows(len_ref, lo_ref, hi_ref, lax.axis_index("seq") + base, modulus)
     run_layers(x_ref, y_ref, gain_ref, bias_ref, taps_ref, w_ref, u_ref, act_ref, lo_ref, hi_ref, layers, shifts, modulus, copies)
 
@@ -147,7 +155,7 @@
         in_specs=[pl.BlockSpec(memory_space=pltpu.SMEM)] + [in_vmem] * 4 + [pl.BlockSpec(memory_space=pltpu.HBM)],
         out_specs=in_vmem,
         scratch_shapes=[
-            pltpu.VMEM((rows + 2 * pad, channels), jnp.float32),
+            pltpu.VMEM((2, rows + 2 * pad, channels), jnp.float32),
             pltpu.VMEM((rows, channels), jnp.bfloat16),
             pltpu.VMEM((rows, LANES), jnp.int32),
             pltpu.VMEM((rows, LANES), jnp.int32),

time: 111 us -> 104 us (0.937)
  Pallas kernels: 47 us -> 39.6 us
  waiting for transfers between devices: 8.08 us -> 12.8 us
  starting transfers between devices: 16.8 us -> 14.5 us
  blocking collectives: 25.2 us -> 23.9 us
    pallas_call x2, Pallas kernels: 43.1 us -> 35.8 us  [local_stack(): pl.pallas_call(functools.partial(stack_kernel, layers, shifts, modulus, b...]
    all_to_all x1, waiting for transfers between devices: 0.01 us -> 2.39 us  [body(): outs.append(lax.all_to_all(done.reshape(count, per, channels), 'seq', 0, 0))]
    all_to_all x2, waiting for transfers between devices: 8.08 us -> 10.5 us  [body(): arrived = lax.all_to_all(part, 'seq', 0, 0)]
    all_to_all x1, starting transfers between devices: 6.01 us -> 3.65 us  [body(): outs.append(lax.all_to_all(done.reshape(count, per, channels), 'seq', 0, 0))]
    all_to_all x1, blocking collectives: 25.2 us -> 23.9 us  [body(): outs.append(lax.all_to_all(done.reshape(count, per, channels), 'seq', 0, 0))]
  transfers between devices with their start and end apart: 3 -> 3, of which waited for: 1 -> 3; matrix products, arithmetic and copies ran while one was open for 4% -> 5% of each run, Pallas kernels for 43% -> 38%
where the time goes in v2:
time: 104 us
  Pallas kernels  39.6 us (38%)
  blocking collectives  23.9 us (23%)
  starting transfers between devices  14.5 us (14%)
  local copies, waits for them, and re-layouts  12.9 us (12%)
  waiting for transfers between devices  12.8 us (12%)
    pallas_call x2, Pallas kernels, local_stack(): pl.pallas_call(functools.partial(stack_kernel, layers, shifts, modulus, b...  35.8 us
    all_to_all x1, blocking collectives, body(): outs.append(lax.all_to_all(done.reshape(count, per, channels), 'seq', 0, 0))  23.9 us
    all_to_all x2, starting transfers between devices, body(): arrived = lax.all_to_all(part, 'seq', 0, 0)  10.8 us
    all_to_all x2, waiting for transfers between devices, body(): arrived = lax.all_to_all(part, 'seq', 0, 0)  10.5 us
    unnamed x12, local copies, waits for them, and re-layouts  9.36 us
    pallas_call x1, Pallas kernels, dense_weights(): pl.pallas_call(functools.partial(weights_kernel, layers), out_shape=jax.S...  3.83 us
    all_to_all x1, starting transfers between devices, body(): outs.append(lax.all_to_all(done.reshape(count, per, channels), 'seq', 0, 0))  3.65 us
    all_to_all x1, waiting for transfers between devices, body(): outs.append(lax.all_to_all(done.reshape(count, per, channels), 'seq', 0, 0))  2.39 us
  transfers between devices with their start and end apart: 3, of which 3 were waited for; matrix products, arithmetic and copies ran while one was open for 5% of the time, Pallas kernels for 38%

profile of v2, /device:TPU:0, one launch (start us, length us, event | category | flops | bytes accessed | tf_op | source)
XLA Modules:
  0.0 103.9 jit_solution(4610777020592223936)
XLA Ops:
  0.0 1.5 %fusion = (bf16[64,8,768]{2,1,0:T(8,128)(2,1)S(1)}, bf16[64,8,768]{2,1,0:T(8,128)(2,1)S(1)}) fusion(bf16[64,16,768]{2,1,0:T(8,128)(2,1)} %bitcast.17), kind=kLoop, calls=%fused_computation.3 | loop fusion | bytes 3145728 | tf_op jit(solution)/shard_map/slice | solution.py:223
  1.5 1.0 %copy.18 = bf16[64,8,768]{2,0,1:T(8,128)(2,1)} copy(bf16[64,8,768]{2,1,0:T(8,128)(2,1)S(1)} %get-tuple-element.9) | data formatting | bytes 1572864
  2.5 7.3 %all-to-all-start = ((bf16[8,64,768]{2,1,0:T(8,128)(2,1)}), bf16[8,64,768]{2,1,0:T(8,128)(2,1)}, u32[]{:S(2)}, u32[]{:S(2)}) async-start(bf16[8,64,768]{2,1,0:T(8,128)(2,1)} %bitcast.12), calls=%async_computation | async-start | bytes 1572864 | tf_op jit(solution)/shard_map/all_to_all | solution.py:227
  9.8 1.0 copy.19
  10.8 0.0 copy-start.3
  10.8 0.0 copy-start.2
  10.8 3.0 %copy.10.pw_ref = bf16[8,768,192]{2,1,0:T(8,128)(2,1)S(1)} copy(bf16[8,768,192]{1,2,0:T(8,128)(2,1)} %param.12) | data formatting | bytes 4718592 | tf_op args[5]
  13.9 0.0 copy-done.3
  13.9 0.0 copy-done.2
  13.9 0.6 copy.11.taps_ref
  14.5 3.8 %shard_map.73.w_hbm = bf16[8,768,768]{2,1,0:T(8,128)(2,1)S(1)} custom-call(bf16[8,768,192]{2,1,0:T(8,128)(2,1)S(1)} %copy.10.pw_ref, s32[8,1,768]{2,1,0:T(1,128)S(1)} %reshape.19.order_ref), custom_call_target="tpu_custom_call" | custom-call | flops 2000000000 | bytes 20000000 | tf_op jit(solution)/shard_map/pallas_call | solution.py:126
  18.4 0.0 copy-start
  18.4 3.6 %copy-done = bf16[8,768,768]{2,1,0:T(8,128)(2,1)} copy-done((bf16[8,768,768]{2,1,0:T(8,128)(2,1)}, bf16[8,768,768]{2,1,0:T(8,128)(2,1)S(1)}, u32[]{:S(2)}) %copy-start) | copy-done | bytes 9437208
  22.0 8.1 %all-to-all-done = bf16[8,64,768]{2,1,0:T(8,128)(2,1)} async-done(((bf16[8,64,768]{2,1,0:T(8,128)(2,1)}), bf16[8,64,768]{2,1,0:T(8,128)(2,1)}, u32[]{:S(2)}, u32[]{:S(2)}) %all-to-all-start) | async-done | bytes 786464 | tf_op jit(solution)/shard_map/all_to_all | solution.py:227
  30.1 3.6 %all-to-all-start.2 = ((bf16[8,64,768]{2,1,0:T(8,128)(2,1)}), bf16[8,64,768]{2,1,0:T(8,128)(2,1)S(1)}, u32[]{:S(2)}, u32[]{:S(2)}) async-start(bf16[8,64,768]{2,1,0:T(8,128)(2,1)} %bitcast.14), calls=%async_computation.2 | async-start | bytes 1572864 | tf_op jit(solution)/shard_map/all_to_all | solution.py:227
  33.6 18.0 %shard_map.74 = bf16[512,768]{1,0:T(8,128)(2,1)} custom-call(s32[1,4]{1,0:T(1,128)} %len_ref.3, bf16[512,768]{1,0:T(8,128)(2,1)} %bitcast.3.x_ref, bf16[8,768]{1,0:T(8,128)(2,1)} %gain_ref.3, bf16[8,768]{1,0:T(8,128)(2,1)} %bias_ref.3, bf16[8,3,768]{2,1,0:T(4,128)(2,1)} %copy.11.taps_ref, bf16[8,768,768]{2,1,0:T(8,128)(2,1)} %copy-done), custom_call_target="tpu_custom_call" | custom-call | flops 20000000000 | bytes 20000000 | tf_op jit(solution)/shard_map/pallas_call | solution.py:152
  51.6 2.4 %all-to-all-done.2 = bf16[8,64,768]{2,1,0:T(8,128)(2,1)S(1)} async-done(((bf16[8,64,768]{2,1,0:T(8,128)(2,1)}), bf16[8,64,768]{2,1,0:T(8,128)(2,1)S(1)}, u32[]{:S(2)}, u32[]{:S(2)}) %all-to-all-start.2) | async-done | bytes 786464 | tf_op jit(solution)/shard_map/all_to_all | solution.py:227
  54.0 0.0 copy-start.1
  54.0 3.7 %all-to-all-start.1 = ((bf16[8,64,768]{2,1,0:T(8,128)(2,1)}), bf16[8,64,768]{2,1,0:T(8,128)(2,1)S(1)}, u32[]{:S(2)}, u32[]{:S(2)}) async-start(bf16[8,64,768]{2,1,0:T(8,128)(2,1)} %bitcast.19), calls=%async_computation.1 | async-start | bytes 1572864 | tf_op jit(solution)/shard_map/all_to_all | solution.py:234
  57.7 0.0 copy-done.1
  57.7 17.8 %shard_map.75 = bf16[512,768]{1,0:T(8,128)(2,1)} custom-call(s32[1,4]{1,0:T(1,128)} %len_ref.3, bf16[512,768]{1,0:T(8,128)(2,1)} %bitcast.18, bf16[8,768]{1,0:T(8,128)(2,1)} %gain_ref.3, bf16[8,768]{1,0:T(8,128)(2,1)} %bias_ref.3, bf16[8,3,768]{2,1,0:T(4,128)(2,1)} %copy.11.taps_ref, bf16[8,768,768]{2,1,0:T(8,128)(2,1)} %copy-done), custom_call_target="tpu_custom_call" | custom-call | flops 20000000000 | bytes 20000000 | tf_op jit(solution)/shard_map/pallas_call | solution.py:152
  75.5 2.4 %all-to-all-done.1 = bf16[8,64,768]{2,1,0:T(8,128)(2,1)S(1)} async-done(((bf16[8,64,768]{2,1,0:T(8,128)(2,1)}), bf16[8,64,768]{2,1,0:T(8,128)(2,1)S(1)}, u32[]{:S(2)}, u32[]{:S(2)}) %all-to-all-start.1) | async-done | bytes 786464 | tf_op jit(solution)/shard_map/all_to_all | solution.py:234
  77.9 23.9 %all_to_all.20 = bf16[8,64,768]{2,1,0:T(8,128)(2,1)S(1)} all-to-all(bf16[8,64,768]{2,1,0:T(8,128)(2,1)} %bitcast.20), channel_id=1, replica_groups=mesh['win'=4,'seq'=8] {'seq'}, dimensions={0} | all-to-all | bytes 1572864 | tf_op jit(solution)/shard_map/all_to_all | solution.py:236
  101.8 0.1 pad_maximum_fusion
  101.9 2.0 %copy.13 = bf16[64,16,768]{2,1,0:T(8,128)(2,1)} copy(bf16[64,16,768]{2,0,1:T(8,128)(2,1)S(1)} %pad_maximum_fusion) | data formatting | bytes 3145728 | tf_op jit(solution)/shard_map/concatenate | solution.py:237
  (1 shorter events, 0.0 us)
Async XLA Ops:
  2.5 27.6 %all-to-all-start = ((bf16[8,64,768]{2,1,0:T(8,128)(2,1)}), bf16[8,64,768]{2,1,0:T(8,128)(2,1)}, u32[]{:S(2)}, u32[]{:S(2)}) async-start(bf16[8,64,768]{2,1,0:T(8,128)(2,1)} %bitcast.12), calls=%async_computation | async-start | bytes 1572864 | tf_op jit(solution)/shard_map/all_to_all | solution.py:227
  10.8 3.0 %copy-start.3 = (s32[8,768]{1,0:T(8,128)S(1)}, s32[8,768]{1,0:T(8,128)}, u32[]{:S(2)}) copy-start(s32[8,768]{1,0:T(8,128)} %param.13) | copy-start | bytes 73732
  10.8 3.1 %copy-start.2 = (bf16[8,3,768]{2,0,1:T(8,128)(2,1)S(1)}, bf16[8,3,768]{2,0,1:T(8,128)(2,1)}, u32[]{:S(2)}) copy-start(bf16[8,3,768]{2,0,1:T(8,128)(2,1)} %param.11) | copy-start | bytes 110596
  18.4 3.6 %copy-start = (bf16[8,768,768]{2,1,0:T(8,128)(2,1)}, bf16[8,768,768]{2,1,0:T(8,128)(2,1)S(1)}, u32[]{:S(2)}) copy-start(bf16[8,768,768]{2,1,0:T(8,128)(2,1)S(1)} %shard_map.73.w_hbm) | copy-start | bytes 28311556
  30.1 23.9 %all-to-all-start.2 = ((bf16[8,64,768]{2,1,0:T(8,128)(2,1)}), bf16[8,64,768]{2,1,0:T(8,128)(2,1)S(1)}, u32[]{:S(2)}, u32[]{:S(2)}) async-start(bf16[8,64,768]{2,1,0:T(8,128)(2,1)} %bitcast.14), calls=%async_computation.2 | async-start | bytes 1572864 | tf_op jit(solution)/shard_map/all_to_all | solution.py:227
  54.0 3.7 %copy-start.1 = (bf16[8,64,768]{2,1,0:T(8,128)(2,1)}, bf16[8,64,768]{2,1,0:T(8,128)(2,1)S(1)}, u32[]{:S(2)}) copy-start(bf16[8,64,768]{2,1,0:T(8,128)(2,1)S(1)} %all-to-all-done.2) | copy-start | bytes 2359300
  54.0 23.9 %all-to-all-start.1 = ((bf16[8,64,768]{2,1,0:T(8,128)(2,1)}), bf16[8,64,768]{2,1,0:T(8,128)(2,1)S(1)}, u32[]{:S(2)}, u32[]{:S(2)}) async-start(bf16[8,64,768]{2,1,0:T(8,128)(2,1)} %bitcast.19), calls=%async_computation.1 | async-start | bytes 1572864 | tf_op jit(solution)/shard_map/all_to_all | solution.py:234
